TPU v7x, 256 devices: a whole 4x4x8 slice. The times are simulated.
256 devices in a mesh: lang: 4 (over x), fsdp: 16 (over z, core), dp: 4 (over y).
Axes of the slice: x: 4, y: 4, z: 8, core: 2. Of those that a mesh axis runs over, the one named last changes fastest.
Arguments:
- tokens_in: bfloat16 [1024, 8192], P('dp'), may hold values from -6 to 6
- cotangent: bfloat16 [1024, 16384], P('dp', ('lang', 'fsdp')), may hold values from -6 to 6
- gate_base: bfloat16 [8192, 16384], P('dp', ('lang', 'fsdp')), may hold values from -0.0625 to 0.0625
- up_base: bfloat16 [8192, 16384], P('dp', ('lang', 'fsdp')), may hold values from -0.0625 to 0.0625
- lang_delta: bfloat16 [4, 16, 4, 4, 32768], P('lang', 'fsdp'), may hold values from -0.1796875 to 0.1796875
- lang_cell: int32 [4, 16, 4, 4], P('lang', 'fsdp'), may hold values from -1 to 127, as said below
- group_lang: int32 [4], P('dp'), may hold values from 0 to 3
- task_delta: bfloat16 [1024, 32768], P(('lang', 'fsdp')), may hold values from -0.1796875 to 0.1796875
- task_slab: int32 [1024, 1], P(('lang', 'fsdp')), may hold values from 0 to 15; in each aligned block of 16 rows (0 to 15, 16 to 31, ...) at most 2 rows name the same one
- task_cell: int32 [1024, 1], P(('lang', 'fsdp')), may hold values from 0 to 127
Outputs:
- grad_input: bfloat16 [1024, 8192], P('dp', ('lang', 'fsdp'))
- task_grad: float32 [1024, 32768], P(('lang', 'fsdp'))
Inputs may be any that keep to these rules, and one draw needn't show every extreme that they name: `lang_cell`: -1 marks an empty slot; every other entry is a cell of the slab. In every draw the list of slab 0 is full for every language. `task_slab`: among the 16 task blocks of one device, no slab is named more than 2 times; some slab is named exactly 2 times.
All inputs are finite; a program needn't handle non-finite values.
Results may differ from a plain program's by a relative error of at most 0.0063.
Values may be sent and summed in bfloat16 or wider, within the bound.
No kernel may reach another device: no remote copies, remote signals or barrier semaphores. Data moves between devices by JAX's collectives and lax.ppermute only.
A program may use at most 128 MiB of HBM per device.

v0:
```python
import jax
import jax.numpy as jnp
from jax import lax
from jax.sharding import PartitionSpec as P

D = 8192
BLK = 128


def spread(value, axis, source):
    kept = jnp.where(lax.axis_index(axis) == source, value, 0).astype(value.dtype)
    return lax.psum(kept, axis)


def place_blocks(cell_ids, tile_vals, cell_total):
    one_hot = (cell_ids[:, None] == jnp.arange(cell_total, dtype=jnp.int32)[None, :]).astype(
        jnp.bfloat16
    )
    return lax.dot_general(
        one_hot, tile_vals, (((0,), (0,)), ((), ())), preferred_element_type=jnp.float32
    )


def on_device(
    tokens_in,
    cotangent,
    gate_base,
    up_base,
    lang_delta,
    lang_cell,
    group_lang,
    task_delta,
    task_slab,
    task_cell,
):
    tile_size = BLK * BLK
    slab_cols = gate_base.shape[1]
    slab_width = slab_cols // BLK
    row_blocks = D // BLK
    group_rows = tokens_in.shape[0]
    language = group_lang[0]
    range_index = lax.axis_index("lang")
    owner_vals, owner_cells = (
        spread(lang_delta, "lang", language),
        spread(lang_cell, "lang", language),
    )
    own_tiles = lax.dynamic_index_in_dim(owner_vals[0, 0], range_index, 0, keepdims=False)
    own_cells = lax.dynamic_index_in_dim(owner_cells[0, 0], range_index, 0, keepdims=False)
    fsdp_ways = lax.axis_size("fsdp")
    held = task_delta.shape[0]
    capacity = max(2, (held + fsdp_ways - 1) // fsdp_ways)
    target = task_slab[:, 0]
    matches = (target[:, None] == jnp.arange(fsdp_ways, dtype=jnp.int32)[None, :]).astype(jnp.int32)
    slot_of = jnp.sum(jnp.cumsum(matches, axis=0) * matches, axis=1) - 1
    send_vals = (
        jnp.zeros((fsdp_ways, capacity, 2 * tile_size), jnp.bfloat16)
        .at[target, slot_of]
        .set(task_delta)
    )
    send_cells = (
        jnp.full((fsdp_ways, capacity), -1, jnp.int32).at[target, slot_of].set(task_cell[:, 0])
    )
    got_vals, got_cells = (
        lax.all_to_all(send_vals, "fsdp", split_axis=0, concat_axis=0, tiled=True),
        lax.all_to_all(send_cells, "fsdp", split_axis=0, concat_axis=0, tiled=True),
    )
    base_gate, base_up = (
        lax.all_gather(gate_base, "dp", axis=0, tiled=True),
        lax.all_gather(up_base, "dp", axis=0, tiled=True),
    )
    slot_cells = got_cells.reshape(-1)
    all_cells = jnp.concatenate([own_cells, slot_cells])
    all_tiles = jnp.concatenate([own_tiles, got_vals.reshape(-1, 2 * tile_size)], axis=0)
    changes = place_blocks(all_cells, all_tiles, row_blocks * slab_width)
    changes = changes.reshape(row_blocks, slab_width, 2, BLK, BLK)

    def as_matrix(part_index):
        return changes[:, :, part_index].transpose(0, 2, 1, 3).reshape(D, slab_cols)

    gate_matrix = (base_gate.astype(jnp.float32) + as_matrix(0)).astype(jnp.bfloat16)
    up_matrix = (base_up.astype(jnp.float32) + as_matrix(1)).astype(jnp.bfloat16)
    gate_pre = jnp.dot(tokens_in, gate_matrix, preferred_element_type=jnp.float32)
    up_pre = jnp.dot(tokens_in, up_matrix, preferred_element_type=jnp.float32)
    sigmoid_g = jax.nn.sigmoid(gate_pre)
    upstream = cotangent.astype(jnp.float32)
    d_gate = (upstream * up_pre * sigmoid_g * (1.0 + gate_pre * (1.0 - sigmoid_g))).astype(
        jnp.bfloat16
    )
    d_up = (upstream * gate_pre * sigmoid_g).astype(jnp.bfloat16)
    contract = (((1,), (1,)), ((), ()))
    partial_g = lax.dot_general(gate_matrix, d_gate, contract, preferred_element_type=jnp.float32)
    summed = lax.psum_scatter(
        partial_g + lax.dot_general(up_matrix, d_up, contract, preferred_element_type=jnp.float32),
        ("lang", "fsdp"),
        scatter_dimension=0,
        tiled=True,
    )
    grad_input = summed.T.astype(jnp.bfloat16)
    filled = slot_cells >= 0
    clamped = jnp.where(filled, slot_cells, 0)
    x_tiles = tokens_in.reshape(group_rows, row_blocks, BLK)[:, clamped // slab_width, :]
    g_tiles = d_gate.reshape(group_rows, slab_width, BLK)[:, clamped % slab_width, :]
    u_tiles = d_up.reshape(group_rows, slab_width, BLK)[:, clamped % slab_width, :]
    gate_grad = jnp.einsum("tmi,tmj->mij", x_tiles, g_tiles, preferred_element_type=jnp.float32)
    up_grad = jnp.einsum("tmi,tmj->mij", x_tiles, u_tiles, preferred_element_type=jnp.float32)
    slot_grads = jnp.concatenate(
        [gate_grad.reshape(-1, tile_size), up_grad.reshape(-1, tile_size)], axis=1
    )
    slot_grads = jnp.where(filled[:, None], slot_grads, 0.0).reshape(
        fsdp_ways, capacity, 2 * tile_size
    )
    slot_grads = lax.psum(slot_grads, "dp")
    returned = lax.all_to_all(slot_grads, "fsdp", split_axis=0, concat_axis=0, tiled=True)
    task_grad = returned[target, slot_of]
    return (grad_input, task_grad)


def solution(mesh):
    return jax.shard_map(
        on_device,
        mesh=mesh,
        in_specs=(
            P("dp", None),
            P("dp", ("lang", "fsdp")),
            P("dp", ("lang", "fsdp")),
            P("dp", ("lang", "fsdp")),
            P("lang", "fsdp", None, None, None),
            P("lang", "fsdp", None, None),
            P("dp"),
            P(("lang", "fsdp"), None),
            P(("lang", "fsdp"), None),
            P(("lang", "fsdp"), None),
        ),
        out_specs=(P("dp", ("lang", "fsdp")), P(("lang", "fsdp"), None)),
        check_vma=False,
    )
```

profile of v0, /device:TPU:9, one launch (start us, length us, event | category | flops | bytes accessed | tf_op | source)
XLA Modules:
  0.0 436.3 jit_solution(2967037532233484744)
XLA Ops:
  13.1 9.2 %all-to-all-start = ((s32[16,1,2]{2,1,0:T(1,128)}), s32[16,1,2]{2,1,0:T(1,128)S(1)}, u32[]{:S(2)}, u32[]{:S(2)}) async-start(s32[16,1,2]{2,1,0:T(1,128)} %copy.56), calls=%async_computation | async-start | bytes 16384 | tf_op jit(solution)/shard_map/all_to_all | solution.py:65
  23.0 7.4 %psum.21 = s32[1,1,4,4]{3,2,1,0:T(4,128)S(1)} all-reduce(s32[1,1,4,4]{3,2,1,0:T(4,128)S(1)} %broadcast_select_fusion.1), channel_id=1, replica_groups=mesh['lang'=4,'fsdp'=16,'dp'=4] {'lang'}, use_global_device_ids=true, to_apply=%region_0.1 | all-reduce | flops 16 | bytes 128 | tf_op jit(solution)/shard_map/psum | solution.py:12
  30.4 6.5 %copy.62 = bf16[256,8192]{0,1:T(8,128)(2,1)} copy(bf16[256,8192]{1,0:T(8,128)(2,1)} %param.10) | data formatting | bytes 8388608 | tf_op args[0]
  36.9 6.5 %copy.63 = bf16[256,64,128]{2,0,1:T(8,128)(2,1)} copy(bf16[256,64,128]{0,2,1:T(8,128)(2,1)} %bitcast.101) | data formatting | bytes 8388608 | tf_op jit(solution)/shard_map/reshape | solution.py:101
  46.3 20.2 %scatter_fusion.1 = bf16[16,2,32768]{2,1,0:T(2,128)(2,1)} fusion(bf16[16,2,32768]{2,1,0:T(2,128)(2,1)} %broadcast_in_dim.44, s32[16]{0:T(128)S(1)} %get-tuple-element.14, bf16[16,32768]{1,0:T(8,128)(2,1)S(1)} %copy-done.4), kind=kCustom, calls=%fused_computation.5 | custom fusion | bytes 3145856 | tf_op jit(solution)/shard_map/scatter | solution.py:58
  66.5 8.8 %all-to-all-start.1 = ((bf16[16,2,32768]{2,1,0:T(2,128)(2,1)}), bf16[16,2,32768]{2,1,0:T(2,128)(2,1)S(1)}, u32[]{:S(2)}, u32[]{:S(2)}) async-start(bf16[16,2,32768]{2,1,0:T(2,128)(2,1)} %scatter_fusion.1), calls=%async_computation.1 | async-start | bytes 4194304 | tf_op jit(solution)/shard_map/all_to_all | solution.py:64
  77.3 4.3 gather_fusion
  82.7 41.6 %all-to-all-done.1 = bf16[16,2,32768]{2,1,0:T(2,128)(2,1)S(1)} async-done(((bf16[16,2,32768]{2,1,0:T(2,128)(2,1)}), bf16[16,2,32768]{2,1,0:T(2,128)(2,1)S(1)}, u32[]{:S(2)}, u32[]{:S(2)}) %all-to-all-start.1) | async-done | bytes 2097184 | tf_op jit(solution)/shard_map/all_to_all | solution.py:64
  126.5 4.0 convolution_bitcast_fusion
  130.6 5.2 %copy.71 = f32[16,8,256,128]{3,2,1,0:T(8,128)S(1)} copy(f32[16,8,256,128]{3,1,2,0:T(8,128)S(1)} %convolution_bitcast_fusion) | data formatting | bytes 33554432
  135.8 6.3 %slice_bitcast_fusion = (f32[64,128,2,128]{3,1,2,0:T(8,128)}, f32[64,128,2,128]{3,1,2,0:T(8,128)}) fusion(f32[64,2,2,128,128]{4,3,2,1,0:T(8,128)S(1)} %bitcast.100), kind=kLoop, calls=%fused_computation.12 | loop fusion | bytes 33554432 | tf_op jit(solution)/shard_map/transpose | solution.py:78
  142.1 15.5 %copy.57 = f32[64,128,2,128]{3,2,1,0:T(2,128)} copy(f32[64,128,2,128]{3,1,2,0:T(8,128)} %get-tuple-element.17) | data formatting | bytes 16777216 | tf_op jit(solution)/shard_map/transpose | solution.py:78
  157.6 7.8 %copy.59 = f32[64,128,2,128]{3,2,1,0:T(2,128)} copy(f32[64,128,2,128]{3,1,2,0:T(8,128)S(1)} %copy-done) | data formatting | bytes 16777216 | tf_op jit(solution)/shard_map/transpose | solution.py:78
  165.4 7.8 %fusion.16 = (bf16[256,256]{0,1:T(8,128)(2,1)S(1)}, f32[256,256]{0,1:T(8,128)S(1)}) fusion(bf16[256,256]{0,1:T(8,128)(2,1)S(1)} %copy.58, bf16[256,8192]{1,0:T(8,128)(2,1)} %param.10, f32[1024,8,2,128]{3,2,1,0:T(2,128)} %bitcast.96, bf16[8192,256]{1,0:T(8,128)(2,1)} %all-gather.3.cloned.1.call-done), kind=kOutput, calls=%fused_computation.33 | convolution fusion | flops 1080492032 | bytes 17301504 | tf_op jit(solution)/shard_map/dot_general | solution.py:82
  175.5 3.7 fusion.5
  182.6 7.8 %fusion.14 = bf16[256,256]{0,1:T(8,128)(2,1)S(1)} fusion(bf16[256,8192]{1,0:T(8,128)(2,1)} %param.10, bf16[256,256]{0,1:T(8,128)(2,1)S(1)} %copy.58, f32[256,256]{0,1:T(8,128)S(1)} %get-tuple-element.19, f32[1024,8,2,128]{3,2,1,0:T(2,128)} %bitcast.98, bf16[8192,256]{1,0:T(8,128)(2,1)} %all-gather.5.cloned.1.call-done), kind=kOutput, calls=%fused_computation.29 | convolution fusion | flops 1080754176 | bytes 17301504 | tf_op jit(solution)/shard_map/dot_general | solution.py:83
  192.7 3.7 fusion.7
  196.4 3.7 concatenate.22
  200.1 6.0 %maximum_select_fusion = f32[16,2,32768]{2,1,0:T(2,128)} fusion(f32[16,2,16384]{2,1,0:T(2,128)S(1)} %copy-done.3, f32[16,2,16384]{2,1,0:T(2,128)} %concatenate.22, pred[16,2]{1,0:T(8,128)(4,1)S(1)} %copy.61), kind=kLoop, calls=%fused_computation.14 | loop fusion | flops 2097152 | bytes 8388640 | tf_op jit(solution)/shard_map/jit(_where)/select_n | solution.py:109
  206.2 6.0 %fusion.24 = f32[8192,256]{1,0:T(8,128)S(1)} fusion(bf16[256,256]{0,1:T(8,128)(2,1)S(1)} %fusion.14, f32[1024,8,2,128]{3,2,1,0:T(2,128)} %bitcast.97, bf16[8192,256]{1,0:T(8,128)(2,1)} %all-gather.3.cloned.1.call-done), kind=kOutput, calls=%fused_computation.66 | convolution fusion | flops 1080033280 | bytes 21102592 | tf_op jit(solution)/shard_map/dot_general | solution.py:91
  212.2 8.9 %convolution_add_fusion = f32[8192,256]{1,0:T(8,128)} fusion(f32[8192,256]{1,0:T(8,128)S(1)} %fusion.24, bf16[256,256]{0,1:T(8,128)(2,1)S(1)} %get-tuple-element.18, f32[1024,8,2,128]{3,2,1,0:T(2,128)} %bitcast.99, bf16[8192,256]{1,0:T(8,128)(2,1)S(1)} %copy-done.2), kind=kOutput, calls=%fused_computation.6 | convolution fusion | flops 1082130432 | bytes 29491200 | tf_op jit(solution)/shard_map/dot_general | solution.py:93
  221.1 79.1 %all-reduce.5.cloned.1.call-done = f32[16,2,32768]{2,1,0:T(2,128)} async-done(((f32[16,2,32768]{2,1,0:T(2,128)}), f32[16,2,32768]{2,1,0:T(2,128)}) %all-reduce.5.cloned.1.call-update) | async-done | bytes 4194320 | tf_op jit(solution)/shard_map/psum | solution.py:112
  300.1 122.0 %all_to_all.19 = f32[16,2,32768]{2,1,0:T(2,128)} all-to-all(f32[16,2,32768]{2,1,0:T(2,128)} %all-reduce.5.cloned.1.call-done), channel_id=1, replica_groups=mesh['lang'=4,'fsdp'=16,'dp'=4] {'fsdp'}, dimensions={0} | all-to-all | bytes 8388608 | tf_op jit(solution)/shard_map/all_to_all | solution.py:113
  422.1 4.9 %gather_fusion.3 = f32[16,32768]{1,0:T(8,128)} fusion(f32[16,2,32768]{2,1,0:T(2,128)} %all_to_all.19, s32[16]{0:T(128)S(1)} %bitcast.104), kind=kCustom, calls=%fused_computation.3 | custom fusion | bytes 4194432 | tf_op jit(solution)/shard_map/gather | solution.py:114
  (66 shorter events, 22.8 us)
Async XLA Ops:
  8.0 2.8 copy-start.6
  8.0 3.1 copy-start.8
  8.0 14.8 %copy-start.5 = (bf16[256,256]{1,0:T(8,128)(2,1)S(1)}, bf16[256,256]{1,0:T(8,128)(2,1)}, u32[]{:S(2)}) copy-start(bf16[256,256]{1,0:T(8,128)(2,1)} %param.11) | copy-start | bytes 393220
  8.0 14.9 %copy-start.7 = (s32[1,1,4,4]{3,2,1,0:T(4,128)S(1)}, s32[1,1,4,4]{3,2,1,0:T(4,128)}, u32[]{:S(2)}) copy-start(s32[1,1,4,4]{3,2,1,0:T(4,128)} %param.15) | copy-start | bytes 196
  8.0 73.6 %all-reduce.3.cloned.1.call-start = ((), (), s32[]{:S(2)}) async-start(), calls=%async_computation.5 | async-start | bytes 2097152 | tf_op jit(solution)/shard_map/psum | solution.py:12
  10.2 155.2 %all-gather.3.cloned.1.call-start = ((), (), s32[]{:S(2)}) async-start(), calls=%async_computation.4 | async-start | bytes 5242880 | tf_op jit(solution)/shard_map/all_gather | solution.py:68
  13.1 53.5 %all-to-all-start = ((s32[16,1,2]{2,1,0:T(1,128)}), s32[16,1,2]{2,1,0:T(1,128)S(1)}, u32[]{:S(2)}, u32[]{:S(2)}) async-start(s32[16,1,2]{2,1,0:T(1,128)} %copy.56), calls=%async_computation | async-start | bytes 16384 | tf_op jit(solution)/shard_map/all_to_all | solution.py:65
  22.2 160.4 %all-gather.5.cloned.1.call-start = ((), (), s32[]{:S(2)}) async-start(), calls=%async_computation.6 | async-start | bytes 5242880 | tf_op jit(solution)/shard_map/all_gather | solution.py:69
  36.9 9.4 %copy-start.4 = (bf16[16,32768]{1,0:T(8,128)(2,1)S(1)}, bf16[16,32768]{1,0:T(8,128)(2,1)}, u32[]{:S(2)}) copy-start(bf16[16,32768]{1,0:T(8,128)(2,1)} %param.17) | copy-start | bytes 3145732
  66.5 57.8 %all-to-all-start.1 = ((bf16[16,2,32768]{2,1,0:T(2,128)(2,1)}), bf16[16,2,32768]{2,1,0:T(2,128)(2,1)S(1)}, u32[]{:S(2)}, u32[]{:S(2)}) async-start(bf16[16,2,32768]{2,1,0:T(2,128)(2,1)} %scatter_fusion.1), calls=%async_computation.1 | async-start | bytes 4194304 | tf_op jit(solution)/shard_map/all_to_all | solution.py:64
  75.4 224.8 %all-reduce.5.cloned.1.call-start = ((), (), s32[]{:S(2)}) async-start(), calls=%async_computation.8 | async-start | bytes 8388608 | tf_op jit(solution)/shard_map/psum | solution.py:112
  142.1 15.5 %copy-start = (f32[64,128,2,128]{3,1,2,0:T(8,128)S(1)}, f32[64,128,2,128]{3,1,2,0:T(8,128)}, u32[]{:S(2)}) copy-start(f32[64,128,2,128]{3,1,2,0:T(8,128)} %get-tuple-element.16) | copy-start | bytes 25165828
  173.2 2.3 copy-start.1
  196.4 3.7 copy-start.3
  206.1 220.9 %reduce-scatter.2.cloned.1.call-start = ((), (), s32[]{:S(2)}) async-start(), calls=%async_computation.7 | async-start | bytes 8519680 | tf_op jit(solution)/shard_map/reduce_scatter | solution.py:92
  206.2 6.0 %copy-start.2 = (bf16[8192,256]{1,0:T(8,128)(2,1)S(1)}, bf16[8192,256]{1,0:T(8,128)(2,1)}, u32[]{:S(2)}) copy-start(bf16[8192,256]{1,0:T(8,128)(2,1)} %all-gather.5.cloned.1.call-done) | copy-start | bytes 12582916
Sparse Core Ops, SparseCore 0:
  11.2 52.1 all-reduce.2
  221.2 187.6 reduce-scatter.1
Sparse Core Ops, SparseCore 1:
  12.6 53.6 all-gather.2
  68.0 51.0 all-gather.4
  206.2 93.9 all-reduce.4
where the time goes:
time: 437 us; the launch traced here: 436 us
  blocking collectives  129 us (30%)
  waiting for transfers between devices  122 us (28%)
  local copies, waits for them, and re-layouts  98.8 us (23%)
  matrix products  41.9 us (10%)
  starting transfers between devices  18.4 us (4%)
  between operations  16.6 us (4%)
  other arithmetic  9.44 us (2%)
    all_to_all x1, blocking collectives, on_device(): lax.all_to_all(slot_grads, 'fsdp', split_axis=0, concat_axis=0, tiled=True)  122 us
    psum x1, waiting for transfers between devices, on_device(): slot_grads = lax.psum(slot_grads, 'dp')  79.1 us
    all_to_all x1, waiting for transfers between devices, on_device(): lax.all_to_all(send_vals, 'fsdp', split_axis=0, concat_axis=0, tiled=True)  41.6 us
    transpose x3, local copies, waits for them, and re-layouts, as_matrix(): return changes[:, :, part_index].transpose(0, 2, 1, 3).reshape(D, slab_cols)  29.6 us
    scatter x1, local copies, waits for them, and re-layouts, on_device(): send_vals = jnp.zeros((fsdp_ways, capacity, 2 * tile_size), jnp.bfloat16)...  20.2 us
    unnamed x22, local copies, waits for them, and re-layouts  12.6 us
    all_to_all x1, starting transfers between devices, on_device(): lax.all_to_all(send_cells, 'fsdp', split_axis=0, concat_axis=0, tiled=True)  9.15 us
    dot_general x1, matrix products, on_device(): lax.dot_general(up_matrix, d_up, contract, preferred_element_type=jnp.flo...  8.88 us
  transfers between devices with their start and end apart: 7, of which 2 were waited for; matrix products, arithmetic and copies ran while one was open for 28% of the time, Pallas kernels for 0%

commit v1 on v0

--- a/solution.py
+++ b/solution.py
@@ -109,7 +109,11 @@
     slot_grads = jnp.where(filled[:, None], slot_grads, 0.0).reshape(
         fsdp_ways, capacity, 2 * tile_size
     )
-    slot_grads = lax.psum(slot_grads, "dp")
+    slot_grads = slot_grads
+    for hop in (1, 2):
+        slot_grads = slot_grads + lax.ppermute(
+            slot_grads, "dp", [(dev, dev ^ hop) for dev in range(4)]
+        )
     returned = lax.all_to_all(slot_grads, "fsdp", split_axis=0, concat_axis=0, tiled=True)
     task_grad = returned[target, slot_of]
     return (grad_input, task_grad)

time: 437 us -> 524 us (1.20); the launches traced: 436 us -> 515 us
  waiting for transfers between devices: 122 us -> 305 us
  blocking collectives: 129 us -> 7.42 us
  other arithmetic: 9.44 us -> 20.1 us
  starting transfers between devices: 18.4 us -> 28.2 us
    ppermute x0 -> x2, waiting for transfers between devices: none -> 170 us  [on_device(): lax.ppermute(slot_grads, 'dp', [(dev, dev ^ hop) for dev in range(4)])]
    all_to_all x1 -> x0, blocking collectives: 122 us -> none  [on_device(): lax.all_to_all(slot_grads, 'fsdp', split_axis=0, concat_axis=0, tiled=True)]
    all_to_all x0 -> x1, waiting for transfers between devices: none -> 91.9 us  [on_device(): lax.all_to_all(slot_grads, 'fsdp', split_axis=0, concat_axis=0, tiled=True)]
    psum x1 -> x0, waiting for transfers between devices: 79.1 us -> none  [on_device(): slot_grads = lax.psum(slot_grads, 'dp')]
    add x0 -> x2, other arithmetic: none -> 9.78 us  [on_device(): slot_grads + lax.ppermute(slot_grads, 'dp', [(dev, dev ^ hop) for dev in...]
    all_to_all x0 -> x1, starting transfers between devices: none -> 6.72 us  [on_device(): lax.all_to_all(slot_grads, 'fsdp', split_axis=0, concat_axis=0, tiled=True)]
    unnamed x22 -> x24, local copies, waits for them, and re-layouts: 12.6 us -> 12.6 us
  transfers between devices with their start and end apart: 7 -> 9, of which waited for: 2 -> 4; matrix products, arithmetic and copies ran while one was open for 28% -> 25% of each run, Pallas kernels for 0% -> 0%
where the time goes in v1:
time: 524 us; the launch traced here: 515 us
  waiting for transfers between devices  305 us (58%)
  local copies, waits for them, and re-layouts  98.9 us (19%)
  matrix products  38.7 us (7%)
  starting transfers between devices  28.2 us (5%)
  other arithmetic  20.1 us (4%)
  between operations  16.7 us (3%)
  blocking collectives  7.42 us (1%)
    ppermute x2, waiting for transfers between devices, on_device(): lax.ppermute(slot_grads, 'dp', [(dev, dev ^ hop) for dev in range(4)])  170 us
    all_to_all x1, waiting for transfers between devices, on_device(): lax.all_to_all(slot_grads, 'fsdp', split_axis=0, concat_axis=0, tiled=True)  91.9 us
    all_to_all x1, waiting for transfers between devices, on_device(): lax.all_to_all(send_vals, 'fsdp', split_axis=0, concat_axis=0, tiled=True)  41.3 us
    transpose x3, local copies, waits for them, and re-layouts, as_matrix(): return changes[:, :, part_index].transpose(0, 2, 1, 3).reshape(D, slab_cols)  29.6 us
    scatter x1, local copies, waits for them, and re-layouts, on_device(): send_vals = jnp.zeros((fsdp_ways, capacity, 2 * tile_size), jnp.bfloat16)...  20.2 us
    unnamed x24, local copies, waits for them, and re-layouts  12.6 us
  transfers between devices with their start and end apart: 9, of which 4 were waited for; matrix products, arithmetic and copies ran while one was open for 25% of the time, Pallas kernels for 0%

profile of v1, /device:TPU:9, one launch (start us, length us, event | category | flops | bytes accessed | tf_op | source)
XLA Modules:
  0.0 514.6 jit_solution(6185661848271464200)
XLA Ops:
  13.1 9.2 %all-to-all-start = ((s32[16,1,2]{2,1,0:T(1,128)}), s32[16,1,2]{2,1,0:T(1,128)S(1)}, u32[]{:S(2)}, u32[]{:S(2)}) async-start(s32[16,1,2]{2,1,0:T(1,128)} %copy.56), calls=%async_computation | async-start | bytes 16384 | tf_op jit(solution)/shard_map/all_to_all | solution.py:65
  23.0 7.4 %psum.14 = s32[1,1,4,4]{3,2,1,0:T(4,128)S(1)} all-reduce(s32[1,1,4,4]{3,2,1,0:T(4,128)S(1)} %broadcast_select_fusion.1), channel_id=1, replica_groups=mesh['lang'=4,'fsdp'=16,'dp'=4] {'lang'}, use_global_device_ids=true, to_apply=%region_0.1 | all-reduce | flops 16 | bytes 128 | tf_op jit(solution)/shard_map/psum | solution.py:12
  30.4 6.5 %copy.62 = bf16[256,8192]{0,1:T(8,128)(2,1)} copy(bf16[256,8192]{1,0:T(8,128)(2,1)} %param.10) | data formatting | bytes 8388608 | tf_op args[0]
  36.9 6.5 %copy.63 = bf16[256,64,128]{2,0,1:T(8,128)(2,1)} copy(bf16[256,64,128]{0,2,1:T(8,128)(2,1)} %bitcast.103) | data formatting | bytes 8388608 | tf_op jit(solution)/shard_map/reshape | solution.py:101
  46.3 20.2 %scatter_fusion.1 = bf16[16,2,32768]{2,1,0:T(2,128)(2,1)} fusion(bf16[16,2,32768]{2,1,0:T(2,128)(2,1)} %broadcast_in_dim.44, s32[16]{0:T(128)S(1)} %get-tuple-element.14, bf16[16,32768]{1,0:T(8,128)(2,1)S(1)} %copy-done.3), kind=kCustom, calls=%fused_computation.5 | custom fusion | bytes 3145856 | tf_op jit(solution)/shard_map/scatter | solution.py:58
  66.6 8.8 %all-to-all-start.1 = ((bf16[16,2,32768]{2,1,0:T(2,128)(2,1)}), bf16[16,2,32768]{2,1,0:T(2,128)(2,1)S(1)}, u32[]{:S(2)}, u32[]{:S(2)}) async-start(bf16[16,2,32768]{2,1,0:T(2,128)(2,1)} %scatter_fusion.1), calls=%async_computation.1 | async-start | bytes 4194304 | tf_op jit(solution)/shard_map/all_to_all | solution.py:64
  77.6 4.3 gather_fusion
  83.0 41.3 %all-to-all-done.1 = bf16[16,2,32768]{2,1,0:T(2,128)(2,1)S(1)} async-done(((bf16[16,2,32768]{2,1,0:T(2,128)(2,1)}), bf16[16,2,32768]{2,1,0:T(2,128)(2,1)S(1)}, u32[]{:S(2)}, u32[]{:S(2)}) %all-to-all-start.1) | async-done | bytes 2097184 | tf_op jit(solution)/shard_map/all_to_all | solution.py:64
  130.6 5.2 %copy.71 = f32[16,8,256,128]{3,2,1,0:T(8,128)S(1)} copy(f32[16,8,256,128]{3,1,2,0:T(8,128)S(1)} %convolution_bitcast_fusion) | data formatting | bytes 33554432
  135.8 6.3 %slice_bitcast_fusion = (f32[64,128,2,128]{3,1,2,0:T(8,128)}, f32[64,128,2,128]{3,1,2,0:T(8,128)}) fusion(f32[64,2,2,128,128]{4,3,2,1,0:T(8,128)S(1)} %bitcast.102), kind=kLoop, calls=%fused_computation.12 | loop fusion | bytes 33554432 | tf_op jit(solution)/shard_map/transpose | solution.py:78
  142.2 15.5 %copy.57 = f32[64,128,2,128]{3,2,1,0:T(2,128)} copy(f32[64,128,2,128]{3,1,2,0:T(8,128)} %get-tuple-element.17) | data formatting | bytes 16777216 | tf_op jit(solution)/shard_map/transpose | solution.py:78
  157.7 7.8 %copy.59 = f32[64,128,2,128]{3,2,1,0:T(2,128)} copy(f32[64,128,2,128]{3,1,2,0:T(8,128)S(1)} %copy-done) | data formatting | bytes 16777216 | tf_op jit(solution)/shard_map/transpose | solution.py:78
  165.5 7.8 %fusion.16 = (bf16[256,256]{0,1:T(8,128)(2,1)S(1)}, f32[256,256]{0,1:T(8,128)S(1)}) fusion(bf16[256,256]{0,1:T(8,128)(2,1)S(1)} %copy.58, bf16[256,8192]{1,0:T(8,128)(2,1)} %param.10, f32[1024,8,2,128]{3,2,1,0:T(2,128)} %bitcast.96, bf16[8192,256]{1,0:T(8,128)(2,1)} %all-gather.3.cloned.1.call-done), kind=kOutput, calls=%fused_computation.33 | convolution fusion | flops 1080492032 | bytes 17301504 | tf_op jit(solution)/shard_map/dot_general | solution.py:82
  182.9 7.8 %fusion.14 = bf16[256,256]{0,1:T(8,128)(2,1)S(1)} fusion(bf16[256,8192]{1,0:T(8,128)(2,1)} %param.10, bf16[256,256]{0,1:T(8,128)(2,1)S(1)} %copy.58, f32[256,256]{0,1:T(8,128)S(1)} %get-tuple-element.19, f32[1024,8,2,128]{3,2,1,0:T(2,128)} %bitcast.98, bf16[8192,256]{1,0:T(8,128)(2,1)} %all-gather.5.cloned.1.call-done), kind=kOutput, calls=%fused_computation.29 | convolution fusion | flops 1080754176 | bytes 17301504 | tf_op jit(solution)/shard_map/dot_general | solution.py:83
  200.2 6.9 %maximum_select_fusion = f32[16,2,32768]{2,1,0:T(2,128)} fusion(f32[16,2,16384]{2,1,0:T(2,128)} %concatenate.23, f32[16,2,16384]{2,1,0:T(2,128)} %concatenate.22, pred[16,2]{1,0:T(8,128)(4,1)S(1)} %copy.61), kind=kLoop, calls=%fused_computation.14 | loop fusion | flops 2097152 | bytes 8388640 | tf_op jit(solution)/shard_map/jit(_where)/select_n | solution.py:109
  207.3 4.8 fusion.24
  212.2 6.8 %convolution_add_fusion = f32[8192,256]{1,0:T(8,128)} fusion(f32[8192,256]{1,0:T(8,128)S(1)} %fusion.24, bf16[256,256]{0,1:T(8,128)(2,1)S(1)} %get-tuple-element.18, f32[1024,8,2,128]{3,2,1,0:T(2,128)S(1)} %bitcast.101, bf16[8192,256]{1,0:T(8,128)(2,1)} %all-gather.5.cloned.1.call-done), kind=kOutput, calls=%fused_computation.6 | convolution fusion | flops 1082130432 | bytes 29491200 | tf_op jit(solution)/shard_map/dot_general | solution.py:93
  219.1 80.2 %collective-permute-done = f32[16,2,32768]{2,1,0:T(2,128)} collective-permute-done((f32[16,2,32768]{2,1,0:T(2,128)}, f32[16,2,32768]{2,1,0:T(2,128)}, u32[]{:S(2)}, u32[]{:S(2)}) %collective-permute-start) | collective-permute-done | bytes 4194336 | tf_op jit(solution)/shard_map/ppermute | solution.py:114
  299.2 5.7 %add.128 = f32[16,2,32768]{2,1,0:T(2,128)S(1)} add(f32[16,2,32768]{2,1,0:T(2,128)} %maximum_select_fusion, f32[16,2,32768]{2,1,0:T(2,128)} %collective-permute-done) | non-fusion elementwise | flops 1048576 | bytes 12582912 | tf_op jit(solution)/shard_map/add | solution.py:114
  307.5 90.1 %collective-permute-done.1 = f32[16,2,32768]{2,1,0:T(2,128)S(1)} collective-permute-done((f32[16,2,32768]{2,1,0:T(2,128)S(1)}, f32[16,2,32768]{2,1,0:T(2,128)S(1)}, u32[]{:S(2)}, u32[]{:S(2)}) %collective-permute-start.1) | collective-permute-done | bytes 4194336 | tf_op jit(solution)/shard_map/ppermute | solution.py:114
  397.6 4.1 add.129
  401.7 6.7 %all-to-all-start.2 = ((f32[16,2,32768]{2,1,0:T(2,128)}), f32[16,2,32768]{2,1,0:T(2,128)}, u32[]{:S(2)}, u32[]{:S(2)}) async-start(f32[16,2,32768]{2,1,0:T(2,128)} %add.129), calls=%async_computation.3 | async-start | bytes 8388608 | tf_op jit(solution)/shard_map/all_to_all | solution.py:117
  410.1 91.9 %all-to-all-done.2 = f32[16,2,32768]{2,1,0:T(2,128)} async-done(((f32[16,2,32768]{2,1,0:T(2,128)}), f32[16,2,32768]{2,1,0:T(2,128)}, u32[]{:S(2)}, u32[]{:S(2)}) %all-to-all-start.2) | async-done | bytes 4194336 | tf_op jit(solution)/shard_map/all_to_all | solution.py:117
  502.0 4.9 gather_fusion.3
  (73 shorter events, 41.0 us)
Async XLA Ops:
  8.0 2.8 copy-start.5
  8.0 3.1 copy-start.7
  8.0 14.8 %copy-start.4 = (bf16[256,256]{1,0:T(8,128)(2,1)S(1)}, bf16[256,256]{1,0:T(8,128)(2,1)}, u32[]{:S(2)}) copy-start(bf16[256,256]{1,0:T(8,128)(2,1)} %param.11) | copy-start | bytes 393220
  8.0 14.9 %copy-start.6 = (s32[1,1,4,4]{3,2,1,0:T(4,128)S(1)}, s32[1,1,4,4]{3,2,1,0:T(4,128)}, u32[]{:S(2)}) copy-start(s32[1,1,4,4]{3,2,1,0:T(4,128)} %param.15) | copy-start | bytes 196
  8.0 73.9 %all-reduce.2.cloned.1.call-start = ((), (), s32[]{:S(2)}) async-start(), calls=%async_computation.5 | async-start | bytes 2097152 | tf_op jit(solution)/shard_map/psum | solution.py:12
  10.2 155.3 %all-gather.3.cloned.1.call-start = ((), (), s32[]{:S(2)}) async-start(), calls=%async_computation.4 | async-start | bytes 5242880 | tf_op jit(solution)/shard_map/all_gather | solution.py:68
  13.1 53.5 %all-to-all-start = ((s32[16,1,2]{2,1,0:T(1,128)}), s32[16,1,2]{2,1,0:T(1,128)S(1)}, u32[]{:S(2)}, u32[]{:S(2)}) async-start(s32[16,1,2]{2,1,0:T(1,128)} %copy.56), calls=%async_computation | async-start | bytes 16384 | tf_op jit(solution)/shard_map/all_to_all | solution.py:65
  22.2 160.6 %all-gather.5.cloned.1.call-start = ((), (), s32[]{:S(2)}) async-start(), calls=%async_computation.6 | async-start | bytes 5242880 | tf_op jit(solution)/shard_map/all_gather | solution.py:69
  36.9 9.4 %copy-start.3 = (bf16[16,32768]{1,0:T(8,128)(2,1)S(1)}, bf16[16,32768]{1,0:T(8,128)(2,1)}, u32[]{:S(2)}) copy-start(bf16[16,32768]{1,0:T(8,128)(2,1)} %param.17) | copy-start | bytes 3145732
  66.6 57.8 %all-to-all-start.1 = ((bf16[16,2,32768]{2,1,0:T(2,128)(2,1)}), bf16[16,2,32768]{2,1,0:T(2,128)(2,1)S(1)}, u32[]{:S(2)}, u32[]{:S(2)}) async-start(bf16[16,2,32768]{2,1,0:T(2,128)(2,1)} %scatter_fusion.1), calls=%async_computation.1 | async-start | bytes 4194304 | tf_op jit(solution)/shard_map/all_to_all | solution.py:64
  75.4 333.1 %reduce-scatter.2.cloned.1.call-start = ((), (), s32[]{:S(2)}) async-start(), calls=%async_computation.7 | async-start | bytes 8519680 | tf_op jit(solution)/shard_map/reduce_scatter | solution.py:92
  142.1 15.5 %copy-start = (f32[64,128,2,128]{3,1,2,0:T(8,128)S(1)}, f32[64,128,2,128]{3,1,2,0:T(8,128)}, u32[]{:S(2)}) copy-start(f32[64,128,2,128]{3,1,2,0:T(8,128)} %get-tuple-element.16) | copy-start | bytes 25165828
  173.2 2.3 copy-start.2
  200.2 7.1 %copy-start.1 = (bf16[8192,256]{1,0:T(8,128)(2,1)S(1)}, bf16[8192,256]{1,0:T(8,128)(2,1)}, u32[]{:S(2)}) copy-start(bf16[8192,256]{1,0:T(8,128)(2,1)} %all-gather.3.cloned.1.call-done) | copy-start | bytes 12582916
  200.2 12.0 %slice-start = ((s8[8388608]{0:T(1024)(128)(4,1)}), s8[4194304]{0:T(1024)(128)(4,1)S(1)}, s32[]{:S(2)}) async-start(s8[8388608]{0:T(1024)(128)(4,1)} %bitcast.99), calls=%async_computation.8 | async-start | bytes 8388608
  207.1 5.1 slice-start.1
  207.1 92.1 %collective-permute-start = (f32[16,2,32768]{2,1,0:T(2,128)}, f32[16,2,32768]{2,1,0:T(2,128)}, u32[]{:S(2)}, u32[]{:S(2)}) collective-permute-start(f32[16,2,32768]{2,1,0:T(2,128)} %maximum_select_fusion), channel_id=1, source_target_pairs={{0,1},{1,0},{2,3},{3,2},{4,5},{5,4},{6,7},{7,6},{8,9},{9,8},{10,11... | collective-permute-start | bytes 12582920 | tf_op jit(solution)/shard_map/ppermute | solution.py:114
  304.9 92.7 %collective-permute-start.1 = (f32[16,2,32768]{2,1,0:T(2,128)S(1)}, f32[16,2,32768]{2,1,0:T(2,128)S(1)}, u32[]{:S(2)}, u32[]{:S(2)}) collective-permute-start(f32[16,2,32768]{2,1,0:T(2,128)S(1)} %add.128), channel_id=1, source_target_pairs={{0,2},{1,3},{2,0},{3,1},{4,6},{5,7},{6,4},{7,5},{8,10},{9,11},{10,... | collective-permute-start | bytes 12582920 | tf_op jit(solution)/shard_map/ppermute | solution.py:114
  401.7 100.3 %all-to-all-start.2 = ((f32[16,2,32768]{2,1,0:T(2,128)}), f32[16,2,32768]{2,1,0:T(2,128)}, u32[]{:S(2)}, u32[]{:S(2)}) async-start(f32[16,2,32768]{2,1,0:T(2,128)} %add.129), calls=%async_computation.3 | async-start | bytes 8388608 | tf_op jit(solution)/shard_map/all_to_all | solution.py:117
Sparse Core Ops, SparseCore 0:
  11.2 52.1 all-reduce.1
  219.2 145.0 reduce-scatter.1
Sparse Core Ops, SparseCore 1:
  12.6 53.6 all-gather.2
  68.0 51.0 all-gather.4
